TPU v7x, 512 devices: a whole 4x8x8 slice. The times are simulated.
512 devices in a mesh: lat: 16 (over x, z_lo, core), lon: 32 (over y, z_hi).
Axes of the slice: x: 4, y: 8, z: 8 (z_hi: 4, z_lo: 2; z = z_hi * 2 + z_lo), core: 2. Of those that a mesh axis runs over, the one named last changes fastest.
Arguments:
- field: bfloat16 [1440, 720, 256], P('lon', 'lat'), may hold values from -6 to 6
- cotangent: bfloat16 [1440, 720, 256], P('lon', 'lat'), may hold values from -6 to 6
- spectral_filter: bfloat16 [2, 720, 256], P(None, None, 'lon'), may hold values from -4 to 4
Outputs:
- output: bfloat16 [1440, 720, 256], P('lon', 'lat')
- grad_field: bfloat16 [1440, 720, 256], P('lon', 'lat')
- grad_filter: float32 [2, 720, 256], P(None, None, 'lon')
All inputs are finite; a program needn't handle non-finite values.
Results may differ from a plain program's by a relative error of at most 0.024.
Values may be sent and summed in bfloat16 or wider, within the bound.
No kernel may reach another device: no remote copies, remote signals or barrier semaphores. Data moves between devices by JAX's collectives and lax.ppermute only.
A program may use at most 128 MiB of HBM per device.

v0:
```python
import math

import jax
import jax.numpy as jnp
from jax import lax
from jax.sharding import PartitionSpec as P


def fourier_table(wave_count, points):
    wave_index = jnp.arange(wave_count, dtype=jnp.int32)
    point_index = jnp.arange(points, dtype=jnp.int32)
    phase_steps = wave_index[:, None] * point_index[None, :] % points
    angles = phase_steps.astype(jnp.float32) * (2.0 * math.pi / points)
    stacked = jnp.stack([jnp.cos(angles), -jnp.sin(angles)], axis=1)
    return stacked.reshape(2 * wave_count, points).astype(jnp.bfloat16)


def compose(earlier, latter):
    upper_left = latter[0] * earlier[0] + latter[1] * earlier[2]
    upper_right = latter[0] * earlier[1] + latter[1] * earlier[3]
    lower_left = latter[2] * earlier[0] + latter[3] * earlier[2]
    lower_right = latter[2] * earlier[1] + latter[3] * earlier[3]
    largest = jnp.maximum(
        jnp.maximum(jnp.abs(upper_left), jnp.abs(upper_right)),
        jnp.maximum(jnp.abs(lower_left), jnp.abs(lower_right)),
    )
    return (
        upper_left / largest,
        upper_right / largest,
        lower_left / largest,
        lower_right / largest,
        earlier[4] + latter[4] + jnp.log(largest),
    )


def legendre_pair(wave_order, lat_count, degree_count):
    order_value = wave_order.astype(jnp.float32)
    degrees = jnp.arange(degree_count, dtype=jnp.float32)
    beyond = degrees > order_value
    numerator = jnp.where(beyond, 4.0 * degrees * degrees - 1.0, 1.0)
    denominator = jnp.where(beyond, degrees * degrees - order_value * order_value, 1.0)
    factor = jnp.sqrt(numerator / denominator)
    earlier_factor = jnp.concatenate([jnp.ones((1,), jnp.float32), factor[:-1]])
    subdiagonal = jnp.where(degrees > order_value + 1.0, -factor / earlier_factor, 0.0)
    start_log = 0.5 * (
        lax.lgamma(order_value + 1.5) - lax.lgamma(jnp.float32(1.5)) - lax.lgamma(order_value + 1.0)
    ) - 0.5 * math.log(4.0 * math.pi)
    colatitude = (jnp.arange(lat_count, dtype=jnp.float32) + 0.5) * (math.pi / lat_count)
    cosine = jnp.cos(colatitude)[None, :]
    sines = jnp.sin(colatitude)
    block_len = 16
    block_count = degree_count // block_len
    grid_shape = (block_count, lat_count)

    def picked(values, step):
        return values.reshape(block_count, block_len)[:, step][:, None]

    def element(step):
        inside = picked(beyond, step)
        return (
            jnp.where(inside, 0.0, 1.0).astype(jnp.float32),
            jnp.where(inside, 1.0, 0.0).astype(jnp.float32),
            picked(subdiagonal, step),
            jnp.where(inside, picked(factor, step) * cosine, 1.0),
            jnp.zeros((block_count, 1), jnp.float32),
        )

    ones_grid = jnp.ones(grid_shape, jnp.float32)
    zeros_grid = jnp.zeros(grid_shape, jnp.float32)
    identity = (ones_grid, zeros_grid, zeros_grid, ones_grid, zeros_grid)
    totals = identity
    for step in range(block_len):
        totals = compose(totals, element(step))
    inclusive = lax.associative_scan(compose, totals, axis=0)
    carry = tuple(
        (
            jnp.concatenate([first[:1], later[:-1]], axis=0)
            for first, later in zip(identity, inclusive)
        )
    )
    lower_parts = []
    log_parts = []
    for step in range(block_len):
        carry = compose(carry, element(step))
        lower_parts.append(carry[3])
        log_parts.append(carry[4])
    lower_right = jnp.stack(lower_parts, axis=1).reshape(degree_count, lat_count)
    log_scale = jnp.stack(log_parts, axis=1).reshape(degree_count, lat_count)
    values = lower_right * jnp.exp(log_scale + start_log + order_value * jnp.log(sines)[None, :])
    functions = jnp.where((degrees >= order_value)[:, None], values, 0.0)
    weights = math.pi / lat_count * sines
    return (functions.astype(jnp.bfloat16), (functions * weights[None, :]).astype(jnp.bfloat16))


def spectral_products(weights, analysis, adjoint_synthesis):
    filter_real = weights[0]
    filter_imaginary = weights[1]
    real_part = filter_real * analysis[0] - filter_imaginary * analysis[1]
    imaginary_part = filter_real * analysis[1] + filter_imaginary * analysis[0]
    filtered = jnp.stack([real_part, imaginary_part]).astype(jnp.bfloat16)
    gradient_term = jnp.stack(
        [
            analysis[0] * adjoint_synthesis[0] + analysis[1] * adjoint_synthesis[1],
            analysis[0] * adjoint_synthesis[1] - analysis[1] * adjoint_synthesis[0],
        ]
    )
    adjoint_filtered = jnp.stack(
        [
            filter_real * adjoint_synthesis[0] + filter_imaginary * adjoint_synthesis[1],
            filter_real * adjoint_synthesis[1] - filter_imaginary * adjoint_synthesis[0],
        ]
    ).astype(jnp.bfloat16)
    return (filtered, gradient_term, adjoint_filtered)


def spectral_work(legendre, weighted, weights, fourier_spec, adjoint_spec):
    analysis = jnp.einsum("lj,rjc->rlc", weighted, fourier_spec, preferred_element_type=jnp.float32)
    adjoint_synthesis = jnp.einsum(
        "lj,rjc->rlc", legendre, adjoint_spec, preferred_element_type=jnp.float32
    )
    filtered, gradient_term, adjoint_filtered = spectral_products(
        weights, analysis, adjoint_synthesis
    )
    synthesis = jnp.einsum(
        "lj,rlc->rjc", legendre, filtered, preferred_element_type=jnp.float32
    ).astype(jnp.bfloat16)
    adjoint_analysis = jnp.einsum(
        "lj,rlc->rjc", weighted, adjoint_filtered, preferred_element_type=jnp.float32
    ).astype(jnp.bfloat16)
    return (synthesis, adjoint_analysis, gradient_term)


def per_device(field, cotangent, spectral_filter):
    lat_count = lax.axis_size("lat")
    lon_count = lax.axis_size("lon")
    lon_local, lat_local, channels = field.shape
    points = lon_local * lon_count
    latitudes = lat_local * lat_count
    wave_count = lat_count * lon_count
    degree_count = spectral_filter.shape[1]
    share_width = lat_local * channels // lon_count
    channel_share = channels // lon_count
    fourier_rows = fourier_table(wave_count, points)
    spacing = 2.0 * math.pi / points
    doubling_rows = jnp.where(jnp.arange(2 * wave_count) // 2 == 0, 1.0, 2.0).astype(jnp.float32)[
        :, None
    ]
    doubling_half = doubling_rows.astype(jnp.bfloat16)

    def transposed_product(columns):
        return lax.dot_general(
            fourier_rows, columns, (((0,), (0,)), ((), ())), preferred_element_type=jnp.float32
        )

    wave_order = lax.axis_index("lon") * lat_count + lax.axis_index("lat")
    legendre, weighted = legendre_pair(wave_order, latitudes, degree_count)
    weights = lax.all_gather(spectral_filter, "lon", axis=2, tiled=True).astype(jnp.float32)

    def wave_blocks(columns):
        return columns.reshape(lon_count, lat_count, 2, 1, 1, share_width)

    def cycle_blocks(spectra):
        return spectra.reshape(1, 1, 2, lat_count, lon_count, share_width)

    def to_columns(grid_values):
        return lax.all_to_all(
            grid_values.reshape(lon_local, lat_local * channels),
            "lon",
            split_axis=1,
            concat_axis=0,
            tiled=True,
        )

    def to_spectral(columns):
        moved = lax.all_to_all(
            lax.all_to_all(wave_blocks(columns), "lat", split_axis=1, concat_axis=3, tiled=True),
            "lon",
            split_axis=0,
            concat_axis=4,
            tiled=True,
        )
        return moved.reshape(2, latitudes, channels)

    def from_spectral(spectra):
        moved = lax.all_to_all(
            lax.all_to_all(cycle_blocks(spectra), "lat", split_axis=3, concat_axis=1, tiled=True),
            "lon",
            split_axis=4,
            concat_axis=0,
            tiled=True,
        )
        return moved.reshape(2 * wave_count, share_width)

    def to_grid(columns):
        return lax.all_to_all(columns, "lon", split_axis=0, concat_axis=1, tiled=True)

    fourier_spec = to_spectral(
        (
            jnp.dot(fourier_rows, to_columns(field), preferred_element_type=jnp.float32) * spacing
        ).astype(jnp.bfloat16)
    )
    adjoint_spec = to_spectral(
        (
            jnp.dot(fourier_rows, to_columns(cotangent), preferred_element_type=jnp.float32)
            * doubling_rows
        ).astype(jnp.bfloat16)
    )
    synthesis, adjoint_analysis, gradient_term = spectral_work(
        legendre, weighted, weights, fourier_spec, adjoint_spec
    )
    output_grid = to_grid(
        transposed_product(doubling_half * from_spectral(synthesis)).astype(jnp.bfloat16)
    )
    gradient_grid = to_grid(
        (transposed_product(from_spectral(adjoint_analysis)) * spacing).astype(jnp.bfloat16)
    )
    summed = lax.psum(gradient_term, ("lat", "lon"))
    grad_filter = lax.dynamic_slice_in_dim(
        summed, lax.axis_index("lon") * channel_share, channel_share, 2
    )
    output = output_grid.reshape(lon_local, lat_local, channels)
    grad_field = gradient_grid.reshape(lon_local, lat_local, channels)
    return (output, grad_field, grad_filter)


def solution(mesh):
    in_specs = (P("lon", "lat", None), P("lon", "lat", None), P(None, None, "lon"))
    out_specs = (P("lon", "lat", None), P("lon", "lat", None), P(None, None, "lon"))
    return jax.shard_map(
        per_device, mesh=mesh, in_specs=in_specs, out_specs=out_specs, check_vma=False
    )
```

profile of v0, /device:TPU:1, one launch (start us, length us, event | category | flops | bytes accessed | tf_op | source)
XLA Modules:
  0.0 775.8 jit_solution(17811050969426552863)
XLA Ops:
  7.2 3.9 all_to_all.169
  12.5 16.7 %all-to-all-start.6 = ((bf16[45,32,360]{2,0,1:T(8,128)(2,1)}), bf16[45,32,360]{2,0,1:T(8,128)(2,1)S(1)}, u32[]{:S(2)}, u32[]{:S(2)}) async-start(bf16[45,32,360]{2,0,1:T(8,128)(2,1)} %copy.121), calls=%async_computation.6 | async-start | bytes 2359296 | tf_op jit(solution)/shard_map/all_to_all | solution.py:166
  37.7 3.6 multiply_add_fusion.88
  57.4 4.1 all_to_all.148
  66.7 12.7 %negate_convert_fusion = (bf16[512,1,1440]{0,2,1:T(8,128)(2,1)S(1)}, bf16[512,1,1440]{0,2,1:T(8,128)(2,1)S(1)}) fusion(), kind=kLoop, calls=%fused_computation.5 | loop fusion | flops 8847360 | bytes 2949120 | tf_op jit(solution)/shard_map/convert.5
  81.3 12.0 %all-to-all-start = ((bf16[45,32,360]{2,0,1:T(8,128)(2,1)}), bf16[45,32,360]{2,0,1:T(8,128)(2,1)}, u32[]{:S(2)}, u32[]{:S(2)}) async-start(bf16[45,32,360]{2,0,1:T(8,128)(2,1)} %copy.95), calls=%async_computation | async-start | bytes 2359296 | tf_op jit(solution)/shard_map/all_to_all | solution.py:166
  93.3 7.4 copy.91
  116.1 4.1 multiply_convert_fusion.2
  123.7 8.2 %all-to-all-start.7 = ((bf16[32,16,2,1,1,360]{5,2,0,4,3,1:T(2,128)(2,1)}), bf16[32,16,2,1,1,360]{5,2,0,4,3,1:T(2,128)(2,1)}, u32[]{:S(2)}, u32[]{:S(2)}) async-start(bf16[32,16,2,1,1,360]{5,2,0,4,3,1:T(2,128)(2,1)} %copy.123), calls=%async_computation.7 | async-start | bytes 1572864 | tf_op jit(solution)/shard_map/all_to_all | solution.py:176
  148.8 5.7 all-to-all-start.1
  168.5 11.0 %all-to-all-start.8 = ((bf16[32,1,2,16,1,360]{5,2,3,4,1,0:T(2,128)(2,1)}), bf16[32,1,2,16,1,360]{5,2,3,4,1,0:T(2,128)(2,1)S(1)}, u32[]{:S(2)}, u32[]{:S(2)}) async-start(bf16[32,1,2,16,1,360]{5,2,3,4,1,0:T(2,128)(2,1)} %copy.124), calls=%async_computation.8 | async-start | bytes 1572864 | tf_op jit(solution)/shard_map/all_to_all | solution.py:175
  189.5 75.4 %all_gather.3 = bf16[2,720,256]{1,0,2:T(2,128)(2,1)S(1)} all-gather(bf16[2,720,8]{1,0,2:T(2,128)(2,1)S(1)} %copy.93), channel_id=1, replica_groups=mesh['lat'=16,'lon'=32] {'lon'}, dimensions={2}, use_global_device_ids=true | all-gather | bytes 760320 | tf_op jit(solution)/shard_map/all_gather | solution.py:157
  268.0 8.6 %stack.159 = f32[45,16,720]{2,1,0:T(8,128)} concatenate(f32[45,1,720]{2,1,0:T(1,128)S(1)} %copy-done.43, f32[45,1,720]{2,1,0:T(1,128)S(1)} %copy-done.44, f32[45,1,720]{2,1,0:T(1,128)S(1)} %copy-done.45, f32[45,1,720]{2,1,0:T(1,128)} %copy.103, f32[45,1,720]{2,1,0:T(1,128)} %copy.104, f32[45,1,720]{2,1,0:T(1,128)} %copy.105, f32[45,1,720]{2,1,0:T(1,128)} %copy.106, ...), dimensions={1} | concatenate | bytes 4147200 | tf_op jit(solution)/shard_map/stack | solution.py:88
  278.0 6.2 all-to-all-start.2
  284.3 5.1 fusion.22
  293.8 3.6 reshape.417
  310.2 3.7 reshape.414
  316.7 19.0 %all-to-all-start.3 = ((bf16[1,1,2,16,32,360]{5,2,4,1,0,3:T(2,128)(2,1)}), bf16[1,1,2,16,32,360]{5,2,4,1,0,3:T(2,128)(2,1)}, u32[]{:S(2)}, u32[]{:S(2)}) async-start(bf16[1,1,2,16,32,360]{5,2,4,1,0,3:T(2,128)(2,1)} %copy.118), calls=%async_computation.3 | async-start | bytes 1572864 | tf_op jit(solution)/shard_map/all_to_all | solution.py:186
  341.7 7.1 all-to-all-done.3
  348.8 4.3 all-to-all-start.9
  355.6 10.5 %all-to-all-done.9 = bf16[1,1,2,16,32,360]{5,2,4,1,0,3:T(2,128)(2,1)S(1)} async-done(((bf16[1,1,2,16,32,360]{5,2,4,1,0,3:T(2,128)(2,1)}), bf16[1,1,2,16,32,360]{5,2,4,1,0,3:T(2,128)(2,1)S(1)}, u32[]{:S(2)}, u32[]{:S(2)}) %all-to-all-start.9) | async-done | bytes 737312 | tf_op jit(solution)/shard_map/all_to_all | solution.py:186
  366.2 8.3 %all-to-all-start.4 = ((bf16[1,16,2,1,32,360]{5,2,1,3,0,4:T(2,128)(2,1)}), bf16[1,16,2,1,32,360]{5,2,1,3,0,4:T(2,128)(2,1)}, u32[]{:S(2)}, u32[]{:S(2)}) async-start(bf16[1,16,2,1,32,360]{5,2,1,3,0,4:T(2,128)(2,1)} %copy.119), calls=%async_computation.4 | async-start | bytes 1572864 | tf_op jit(solution)/shard_map/all_to_all | solution.py:185
  375.9 20.9 %all-to-all-done.4 = bf16[1,16,2,1,32,360]{5,2,1,3,0,4:T(2,128)(2,1)} async-done(((bf16[1,16,2,1,32,360]{5,2,1,3,0,4:T(2,128)(2,1)}), bf16[1,16,2,1,32,360]{5,2,1,3,0,4:T(2,128)(2,1)}, u32[]{:S(2)}, u32[]{:S(2)}) %all-to-all-start.4) | async-done | bytes 737312 | tf_op jit(solution)/shard_map/all_to_all | solution.py:185
  396.9 7.0 all-to-all-start.10
  409.7 3.8 convolution_convert_fusion
  415.9 8.4 %all-to-all-done.10 = bf16[1,16,2,1,32,360]{5,2,1,3,0,4:T(2,128)(2,1)} async-done(((bf16[1,16,2,1,32,360]{5,2,1,3,0,4:T(2,128)(2,1)}), bf16[1,16,2,1,32,360]{5,2,1,3,0,4:T(2,128)(2,1)}, u32[]{:S(2)}, u32[]{:S(2)}) %all-to-all-start.10) | async-done | bytes 737312 | tf_op jit(solution)/shard_map/all_to_all | solution.py:185
  424.3 10.0 %all-to-all-start.5 = ((bf16[32,45,360]{2,1,0:T(8,128)(2,1)}), bf16[32,45,360]{2,1,0:T(8,128)(2,1)S(1)}, u32[]{:S(2)}, u32[]{:S(2)}) async-start(bf16[32,45,360]{2,1,0:T(8,128)(2,1)} %all_to_all.166), calls=%async_computation.5 | async-start | bytes 2359296 | tf_op jit(solution)/shard_map/all_to_all | solution.py:195
  441.4 22.7 %all-to-all-done.5 = bf16[32,45,360]{2,1,0:T(8,128)(2,1)S(1)} async-done(((bf16[32,45,360]{2,1,0:T(8,128)(2,1)}), bf16[32,45,360]{2,1,0:T(8,128)(2,1)S(1)}, u32[]{:S(2)}, u32[]{:S(2)}) %all-to-all-start.5) | async-done | bytes 1036832 | tf_op jit(solution)/shard_map/all_to_all | solution.py:195
  464.1 7.9 %all-to-all-start.11 = ((bf16[32,45,360]{2,1,0:T(8,128)(2,1)}), bf16[32,45,360]{2,1,0:T(8,128)(2,1)S(1)}, u32[]{:S(2)}, u32[]{:S(2)}) async-start(bf16[32,45,360]{2,1,0:T(8,128)(2,1)} %all_to_all.187), calls=%async_computation.11 | async-start | bytes 2359296 | tf_op jit(solution)/shard_map/all_to_all | solution.py:195
  474.5 284.2 %all-reduce.57.cloned.1.call-done = f32[2,720,256]{2,1,0:T(8,128)} async-done(((f32[2,720,256]{2,1,0:T(8,128)}), f32[2,720,256]{2,1,0:T(8,128)}) %all-reduce.57.cloned.1.call-update) | async-done | bytes 1474576 | tf_op jit(solution)/shard_map/psum | solution.py:217
  761.2 3.7 reshape.415
  765.1 3.7 reshape.420
  (547 shorter events, 144.3 us)
Async XLA Ops:
  12.5 68.7 %all-to-all-start.6 = ((bf16[45,32,360]{2,0,1:T(8,128)(2,1)}), bf16[45,32,360]{2,0,1:T(8,128)(2,1)S(1)}, u32[]{:S(2)}, u32[]{:S(2)}) async-start(bf16[45,32,360]{2,0,1:T(8,128)(2,1)} %copy.121), calls=%async_computation.6 | async-start | bytes 2359296 | tf_op jit(solution)/shard_map/all_to_all | solution.py:166
  30.2 14.8 %copy-start.104 = (f32[45]{0:T(128)}, f32[45]{0:T(128)S(1)}, u32[]{:S(2)}) copy-start(f32[45]{0:T(128)S(1)} %get-tuple-element.52) | copy-start | bytes 544
  30.2 16.6 %copy-start.52 = (f32[45]{0:T(128)}, f32[45]{0:T(128)S(1)}, u32[]{:S(2)}) copy-start(f32[45]{0:T(128)S(1)} %get-tuple-element.63) | copy-start | bytes 544
  30.2 16.6 %copy-start.54 = (f32[45]{0:T(128)}, f32[45]{0:T(128)S(1)}, u32[]{:S(2)}) copy-start(f32[45]{0:T(128)S(1)} %get-tuple-element.67) | copy-start | bytes 544
  30.2 16.6 %copy-start.58 = (f32[45]{0:T(128)}, f32[45]{0:T(128)S(1)}, u32[]{:S(2)}) copy-start(f32[45]{0:T(128)S(1)} %get-tuple-element.64) | copy-start | bytes 544
  30.2 16.6 %copy-start.60 = (f32[45]{0:T(128)}, f32[45]{0:T(128)S(1)}, u32[]{:S(2)}) copy-start(f32[45]{0:T(128)S(1)} %get-tuple-element.66) | copy-start | bytes 544
  32.2 14.6 %copy-start.77 = (pred[45]{0:T(512)(128)(4,1)}, pred[45]{0:T(512)(128)(4,1)S(1)}, u32[]{:S(2)}) copy-start(pred[45]{0:T(512)(128)(4,1)S(1)} %get-tuple-element.93) | copy-start | bytes 139
  32.2 14.6 %copy-start.78 = (pred[45]{0:T(512)(128)(4,1)}, pred[45]{0:T(512)(128)(4,1)S(1)}, u32[]{:S(2)}) copy-start(pred[45]{0:T(512)(128)(4,1)S(1)} %get-tuple-element.94) | copy-start | bytes 139
  32.2 14.6 %copy-start.79 = (pred[45]{0:T(512)(128)(4,1)}, pred[45]{0:T(512)(128)(4,1)S(1)}, u32[]{:S(2)}) copy-start(pred[45]{0:T(512)(128)(4,1)S(1)} %get-tuple-element.95) | copy-start | bytes 139
  32.2 14.6 %copy-start.81 = (pred[45]{0:T(512)(128)(4,1)}, pred[45]{0:T(512)(128)(4,1)S(1)}, u32[]{:S(2)}) copy-start(pred[45]{0:T(512)(128)(4,1)S(1)} %get-tuple-element.96) | copy-start | bytes 139
  32.2 14.6 %copy-start.83 = (pred[45]{0:T(512)(128)(4,1)}, pred[45]{0:T(512)(128)(4,1)S(1)}, u32[]{:S(2)}) copy-start(pred[45]{0:T(512)(128)(4,1)S(1)} %get-tuple-element.97) | copy-start | bytes 139
  64.7 14.6 %copy-start.26 = (f32[45,720]{1,0:T(8,128)}, f32[45,720]{1,0:T(8,128)S(1)}, u32[]{:S(2)}) copy-start(f32[45,720]{1,0:T(8,128)S(1)} %get-tuple-element.188) | copy-start | bytes 388804
  66.7 40.3 %copy-start.15 = (f32[45,720]{1,0:T(8,128)}, f32[45,720]{1,0:T(8,128)S(1)}, u32[]{:S(2)}) copy-start(f32[45,720]{1,0:T(8,128)S(1)} %get-tuple-element.175) | copy-start | bytes 388804
  81.3 42.4 %all-to-all-start = ((bf16[45,32,360]{2,0,1:T(8,128)(2,1)}), bf16[45,32,360]{2,0,1:T(8,128)(2,1)}, u32[]{:S(2)}, u32[]{:S(2)}) async-start(bf16[45,32,360]{2,0,1:T(8,128)(2,1)} %copy.95), calls=%async_computation | async-start | bytes 2359296 | tf_op jit(solution)/shard_map/all_to_all | solution.py:166
  115.5 16.4 %copy-start.21 = (f32[45,720]{1,0:T(8,128)}, f32[45,720]{1,0:T(8,128)S(1)}, u32[]{:S(2)}) copy-start(f32[45,720]{1,0:T(8,128)S(1)} %get-tuple-element.139) | copy-start | bytes 388804
  123.7 25.1 %all-to-all-start.7 = ((bf16[32,16,2,1,1,360]{5,2,0,4,3,1:T(2,128)(2,1)}), bf16[32,16,2,1,1,360]{5,2,0,4,3,1:T(2,128)(2,1)}, u32[]{:S(2)}, u32[]{:S(2)}) async-start(bf16[32,16,2,1,1,360]{5,2,0,4,3,1:T(2,128)(2,1)} %copy.123), calls=%async_computation.7 | async-start | bytes 1572864 | tf_op jit(solution)/shard_map/all_to_all | solution.py:176
  148.8 19.7 %all-to-all-start.1 = ((bf16[32,16,2,1,1,360]{5,2,0,4,3,1:T(2,128)(2,1)}), bf16[32,16,2,1,1,360]{5,2,0,4,3,1:T(2,128)(2,1)S(1)}, u32[]{:S(2)}, u32[]{:S(2)}) async-start(bf16[32,16,2,1,1,360]{5,2,0,4,3,1:T(2,128)(2,1)} %copy.97), calls=%async_computation.1 | async-start | bytes 1572864 | tf_op jit(solution)/shard_map/all_to_all | solution.py:176
  164.3 16.0 %copy-start.28 = (f32[45,720]{1,0:T(8,128)S(1)}, f32[45,720]{1,0:T(8,128)}, u32[]{:S(2)}) copy-start(f32[45,720]{1,0:T(8,128)} %get-tuple-element.196) | copy-start | bytes 388804
  168.5 109.5 %all-to-all-start.8 = ((bf16[32,1,2,16,1,360]{5,2,3,4,1,0:T(2,128)(2,1)}), bf16[32,1,2,16,1,360]{5,2,3,4,1,0:T(2,128)(2,1)S(1)}, u32[]{:S(2)}, u32[]{:S(2)}) async-start(bf16[32,1,2,16,1,360]{5,2,3,4,1,0:T(2,128)(2,1)} %copy.124), calls=%async_computation.8 | async-start | bytes 1572864 | tf_op jit(solution)/shard_map/all_to_all | solution.py:175
  189.4 78.5 %copy-start.43 = (f32[45,1,720]{2,1,0:T(1,128)S(1)}, f32[45,1,720]{2,1,0:T(1,128)}, u32[]{:S(2)}) copy-start(f32[45,1,720]{2,1,0:T(1,128)} %copy.100) | copy-start | bytes 388804
  189.4 78.5 %copy-start.44 = (f32[45,1,720]{2,1,0:T(1,128)S(1)}, f32[45,1,720]{2,1,0:T(1,128)}, u32[]{:S(2)}) copy-start(f32[45,1,720]{2,1,0:T(1,128)} %copy.101) | copy-start | bytes 388804
  189.5 78.5 %copy-start.45 = (f32[45,1,720]{2,1,0:T(1,128)S(1)}, f32[45,1,720]{2,1,0:T(1,128)}, u32[]{:S(2)}) copy-start(f32[45,1,720]{2,1,0:T(1,128)} %copy.102) | copy-start | bytes 388804
  278.0 22.4 %all-to-all-start.2 = ((bf16[32,1,2,16,1,360]{5,2,3,4,1,0:T(2,128)(2,1)}), bf16[32,1,2,16,1,360]{5,2,3,4,1,0:T(2,128)(2,1)S(1)}, u32[]{:S(2)}, u32[]{:S(2)}) async-start(bf16[32,1,2,16,1,360]{5,2,3,4,1,0:T(2,128)(2,1)} %copy.98), calls=%async_computation.2 | async-start | bytes 1572864 | tf_op jit(solution)/shard_map/all_to_all | solution.py:175
  316.7 32.1 %all-to-all-start.3 = ((bf16[1,1,2,16,32,360]{5,2,4,1,0,3:T(2,128)(2,1)}), bf16[1,1,2,16,32,360]{5,2,4,1,0,3:T(2,128)(2,1)}, u32[]{:S(2)}, u32[]{:S(2)}) async-start(bf16[1,1,2,16,32,360]{5,2,4,1,0,3:T(2,128)(2,1)} %copy.118), calls=%async_computation.3 | async-start | bytes 1572864 | tf_op jit(solution)/shard_map/all_to_all | solution.py:186
  348.8 17.3 %all-to-all-start.9 = ((bf16[1,1,2,16,32,360]{5,2,4,1,0,3:T(2,128)(2,1)}), bf16[1,1,2,16,32,360]{5,2,4,1,0,3:T(2,128)(2,1)S(1)}, u32[]{:S(2)}, u32[]{:S(2)}) async-start(bf16[1,1,2,16,32,360]{5,2,4,1,0,3:T(2,128)(2,1)} %copy.127), calls=%async_computation.9 | async-start | bytes 1572864 | tf_op jit(solution)/shard_map/all_to_all | solution.py:186
  366.2 30.7 %all-to-all-start.4 = ((bf16[1,16,2,1,32,360]{5,2,1,3,0,4:T(2,128)(2,1)}), bf16[1,16,2,1,32,360]{5,2,1,3,0,4:T(2,128)(2,1)}, u32[]{:S(2)}, u32[]{:S(2)}) async-start(bf16[1,16,2,1,32,360]{5,2,1,3,0,4:T(2,128)(2,1)} %copy.119), calls=%async_computation.4 | async-start | bytes 1572864 | tf_op jit(solution)/shard_map/all_to_all | solution.py:185
  375.9 33.8 %copy-start.5 = (bf16[1024,1440]{1,0:T(8,128)(2,1)S(1)}, bf16[1024,1440]{1,0:T(8,128)(2,1)}, u32[]{:S(2)}) copy-start(bf16[1024,1440]{1,0:T(8,128)(2,1)} %convert_element_type.107) | copy-start | bytes 8847364
  396.9 27.4 %all-to-all-start.10 = ((bf16[1,16,2,1,32,360]{5,2,1,3,0,4:T(2,128)(2,1)}), bf16[1,16,2,1,32,360]{5,2,1,3,0,4:T(2,128)(2,1)}, u32[]{:S(2)}, u32[]{:S(2)}) async-start(bf16[1,16,2,1,32,360]{5,2,1,3,0,4:T(2,128)(2,1)} %copy.128), calls=%async_computation.10 | async-start | bytes 1572864 | tf_op jit(solution)/shard_map/all_to_all | solution.py:185
  424.3 39.8 %all-to-all-start.5 = ((bf16[32,45,360]{2,1,0:T(8,128)(2,1)}), bf16[32,45,360]{2,1,0:T(8,128)(2,1)S(1)}, u32[]{:S(2)}, u32[]{:S(2)}) async-start(bf16[32,45,360]{2,1,0:T(8,128)(2,1)} %all_to_all.166), calls=%async_computation.5 | async-start | bytes 2359296 | tf_op jit(solution)/shard_map/all_to_all | solution.py:195
  440.2 31.9 %copy-start.6 = (f32[1,720,256]{2,1,0:T(8,128)S(1)}, f32[1,720,256]{2,1,0:T(8,128)}, u32[]{:S(2)}) copy-start(f32[1,720,256]{2,1,0:T(8,128)} %get-tuple-element.301) | copy-start | bytes 2211844
  464.1 300.8 %all-to-all-start.11 = ((bf16[32,45,360]{2,1,0:T(8,128)(2,1)}), bf16[32,45,360]{2,1,0:T(8,128)(2,1)S(1)}, u32[]{:S(2)}, u32[]{:S(2)}) async-start(bf16[32,45,360]{2,1,0:T(8,128)(2,1)} %all_to_all.187), calls=%async_computation.11 | async-start | bytes 2359296 | tf_op jit(solution)/shard_map/all_to_all | solution.py:195
  472.0 286.7 %all-reduce.57.cloned.1.call-start = ((), (), s32[]{:S(2)}) async-start(), calls=%async_computation.12 | async-start | bytes 2949120 | tf_op jit(solution)/shard_map/psum | solution.py:217
  (109 other events, 800.4 us)
Sparse Core Ops, SparseCore 0:
  477.8 280.8 all-reduce.56
where the time goes:
time: 781 us; the launch traced here: 776 us
  waiting for transfers between devices  357 us (46%)
  starting transfers between devices  116 us (15%)
  local copies, waits for them, and re-layouts  114 us (15%)
  blocking collectives  75.4 us (10%)
  other arithmetic  75 us (10%)
  matrix products  20.6 us (3%)
  between operations  18.1 us (2%)
    psum x1, waiting for transfers between devices, per_device(): summed = lax.psum(gradient_term, ('lat', 'lon'))  284 us
    all_gather x1, blocking collectives, per_device(): lax.all_gather(spectral_filter, 'lon', axis=2, tiled=True)  75.4 us
    all_to_all x2, waiting for transfers between devices, from_spectral(): lax.all_to_all(lax.all_to_all(cycle_blocks(spectra), 'lat', split_axis=3,...  29.3 us
    all_to_all x2, starting transfers between devices, to_columns(): lax.all_to_all(grid_values.reshape(lon_local, lat_local * channels), 'lon...  28.7 us
    all_to_all x2, starting transfers between devices, from_spectral(): lax.all_to_all(cycle_blocks(spectra), 'lat', split_axis=3, concat_axis=1,...  23.2 us
    all_to_all x2, waiting for transfers between devices, to_grid(): lax.all_to_all(columns, 'lon', split_axis=0, concat_axis=1, tiled=True)  22.7 us
    unnamed x15, other arithmetic  22 us
    another operation x17, local copies, waits for them, and re-layouts, legendre_pair(): log_scale = jnp.stack(log_parts, axis=1).reshape(degree_count, lat_count)  21.3 us
  transfers between devices with their start and end apart: 13, of which 7 were waited for; matrix products, arithmetic and copies ran while one was open for 22% of the time, Pallas kernels for 0%

commit v1 on v0

v1 whole, which is shorter than its diff:
```python
import functools
import math

import jax
import jax.numpy as jnp
from jax import lax
from jax.experimental import pallas as pl
from jax.experimental.pallas import tpu as pltpu
from jax.sharding import PartitionSpec as P

LAT, LON = 16, 32
NLOC, JLOC = 45, 45
NPAD, JPAD = 48, 48
CH = 8
NT = NPAD // 16
KDIM = LON * NPAD
MUDIM = 1024
GROUPS, TG = 4, 8
JALL = LAT * JPAD
DEG, LPAD = 720, 768
POINTS = NLOC * LON
F32, BF16 = jnp.float32, jnp.bfloat16
MIB = 1 << 20


def exchange(tiles, tile_bit, lane_bit):
    step = 1 << lane_bit
    lane = lax.broadcasted_iota(jnp.int32, tiles[0].shape, 1)
    low = (lane & step) == 0
    out = list(tiles)
    for first in range(len(tiles)):
        second = first | (1 << tile_bit)
        if second == first:
            continue
        a, b = tiles[first], tiles[second]
        out[first] = jnp.where(low, a, pltpu.roll(b, step, 1))
        out[second] = jnp.where(low, pltpu.roll(a, 128 - step, 1), b)
    return out


def cost(flops, size):
    return pl.CostEstimate(flops=int(flops), bytes_accessed=int(size), transcendentals=0)


def params(mib):
    return pltpu.CompilerParams(vmem_limit_bytes=mib * MIB)


def share_kernel(x_ref, o_ref):
    def body(nt, jr):
        rows = pl.ds(pl.multiple_of(jr * 16, 16), 16)
        for h in range(2):
            tiles = [
                x_ref[nt * 16 + n, rows, h * 128 : h * 128 + 128].astype(F32) for n in range(16)
            ]
            for b in range(4):
                tiles = exchange(tiles, b, 3 + b)
            for k in range(16):
                o_ref[h * 16 + k, nt, rows, :] = tiles[k].astype(BF16)

    @pl.loop(0, NT * 3)
    def _(s):
        body(s // 3, s % 3)


def to_shares(grid):
    padded = jnp.pad(grid, ((0, NPAD - NLOC), (0, JPAD - JLOC), (0, 0)))
    return pl.pallas_call(
        share_kernel,
        out_shape=jax.ShapeDtypeStruct((LON, NT, JPAD, 128), BF16),
        in_specs=[pl.BlockSpec(memory_space=pltpu.VMEM)],
        out_specs=pl.BlockSpec(memory_space=pltpu.VMEM),
        compiler_params=params(32),
        cost_estimate=cost(1e7, 2.4e6),
        name="to_shares",
    )(padded)


def unshare_kernel(x_ref, o_ref):
    for nt in range(NT):
        for jr in range(3):
            rows = pl.ds(jr * 16, 16)
            count = min(16, JLOC - jr * 16)
            for h in range(2):
                tiles = [x_ref[h * 16 + k, nt, rows, :].astype(F32) for k in range(16)]
                for b in range(4):
                    tiles = exchange(tiles, b, 3 + b)
                for n in range(min(16, NLOC - nt * 16)):
                    o_ref[nt * 16 + n, jr * 16 : jr * 16 + count, h * 128 : h * 128 + 128] = (
                        tiles[n].astype(BF16)[:count]
                    )


def from_shares(shares):
    return pl.pallas_call(
        unshare_kernel,
        out_shape=jax.ShapeDtypeStruct((NLOC, JLOC, 256), BF16),
        in_specs=[pl.BlockSpec(memory_space=pltpu.VMEM)],
        out_specs=pl.BlockSpec(memory_space=pltpu.VMEM),
        compiler_params=params(32),
        cost_estimate=cost(1e7, 2.4e6),
        name="from_shares",
    )(shares)


def fourier_kernel(x_ref, f_ref, row_ref, lane_ref, o_ref, xs_ref, ys_ref):
    @pl.loop(0, 3 * (KDIM // 128))
    def _(s):
        jr, q8 = s // (KDIM // 128), s % (KDIM // 128)
        rows = pl.ds(pl.multiple_of(jr * 16, 16), 16)
        tiles = [x_ref[q8 * 8 + q, rows, :].astype(F32) for q in range(8)]
        for b in range(3):
            tiles = exchange(tiles, b, b)
        lanes = pl.ds(pl.multiple_of(q8 * 128, 128), 128)
        for c in range(8):
            xs_ref[pl.ds(pl.multiple_of(jr * 128 + c * 16, 16), 16), lanes] = tiles[c].astype(BF16)

    ys_ref[...] = jnp.dot(xs_ref[...], f_ref[...], preferred_element_type=F32)

    @pl.loop(0, 3 * 8)
    def _(s):
        jr, ii = s // 8, s % 8
        rows = pl.ds(pl.multiple_of(jr * 16, 16), 16)
        lanes = pl.ds(pl.multiple_of(ii * 128, 128), 128)
        scale = row_ref[rows, :] * lane_ref[:, lanes]
        tiles = [
            ys_ref[pl.ds(pl.multiple_of(jr * 128 + c * 16, 16), 16), lanes] * scale
            for c in range(8)
        ]
        for b in range(3):
            tiles = exchange(tiles, b, 4 + b)
        for i_lo in range(2):
            for g in range(GROUPS):
                o_ref[ii * 2 + i_lo, g, rows, :] = tiles[i_lo * 4 + g].astype(BF16)


def to_waves(shares, table, row_scale, lane_scale):
    return pl.pallas_call(
        fourier_kernel,
        out_shape=jax.ShapeDtypeStruct((LAT, GROUPS, JPAD, 128), BF16),
        in_specs=[pl.BlockSpec(memory_space=pltpu.VMEM)] * 4,
        out_specs=pl.BlockSpec(memory_space=pltpu.VMEM),
        scratch_shapes=[
            pltpu.VMEM((CH * JPAD, KDIM), BF16),
            pltpu.VMEM((CH * JPAD, MUDIM), F32),
        ],
        compiler_params=params(32),
        cost_estimate=cost(2 * 384 * KDIM * MUDIM, 5e6),
        name="to_waves",
    )(shares.reshape(LON * NT, JPAD, 128), table, row_scale, lane_scale)


def inverse_kernel(v_ref, f_ref, row_ref, lane_ref, o_ref, vs_ref, ys_ref):
    @pl.loop(0, 3 * 8)
    def _(s):
        jr, ii = s // 8, s % 8
        rows = pl.ds(pl.multiple_of(jr * 16, 16), 16)
        lanes = pl.ds(pl.multiple_of(ii * 128, 128), 128)
        tiles = [
            v_ref[ii * 2 + i_lo, g, rows, :].astype(F32) for i_lo in range(2) for g in range(GROUPS)
        ]
        for b in range(3):
            tiles = exchange(tiles, b, 4 + b)
        scale = lane_ref[:, lanes]
        for c in range(8):
            vs_ref[pl.ds(pl.multiple_of(jr * 128 + c * 16, 16), 16), lanes] = (
                tiles[c] * scale
            ).astype(BF16)

    ys_ref[...] = lax.dot_general(
        vs_ref[...], f_ref[...], (((1,), (1,)), ((), ())), preferred_element_type=F32
    )

    @pl.loop(0, 3 * (KDIM // 128))
    def _(s):
        jr, q8 = s // (KDIM // 128), s % (KDIM // 128)
        rows = pl.ds(pl.multiple_of(jr * 16, 16), 16)
        lanes = pl.ds(pl.multiple_of(q8 * 128, 128), 128)
        scale = row_ref[rows, :]
        tiles = [
            ys_ref[pl.ds(pl.multiple_of(jr * 128 + c * 16, 16), 16), lanes] * scale
            for c in range(8)
        ]
        for b in range(3):
            tiles = exchange(tiles, b, b)
        for q in range(8):
            o_ref[q8 * 8 + q, rows, :] = tiles[q].astype(BF16)


def from_waves(waves, table, row_scale, lane_scale):
    return pl.pallas_call(
        inverse_kernel,
        out_shape=jax.ShapeDtypeStruct((LON * NT, JPAD, 128), BF16),
        in_specs=[pl.BlockSpec(memory_space=pltpu.VMEM)] * 4,
        out_specs=pl.BlockSpec(memory_space=pltpu.VMEM),
        scratch_shapes=[
            pltpu.VMEM((CH * JPAD, MUDIM), BF16),
            pltpu.VMEM((CH * JPAD, KDIM), F32),
        ],
        compiler_params=params(32),
        cost_estimate=cost(2 * 384 * KDIM * MUDIM, 5e6),
        name="from_waves",
    )(waves, table, row_scale, lane_scale).reshape(LON, NT, JPAD, 128)


LCHUNK = 128


def legendre_kernel(m_ref, f_ref, h_ref, x_ref, p0_ref, e0_ref, o_ref, p1_s, p2_s, e_s, rows_s):
    g, lc = pl.program_id(0), pl.program_id(1)

    @pl.when(lc == 0)
    def _():
        p1_s[...] = jnp.zeros_like(p1_s)
        p2_s[...] = jnp.zeros_like(p2_s)
        e_s[...] = e0_ref[0]

    @pl.when(lc < g)
    def _():
        o_ref[...] = jnp.zeros_like(o_ref)

    @pl.when(lc >= g)
    def _():
        x = jnp.broadcast_to(x_ref[...], (TG, JALL))
        orders = jnp.broadcast_to(m_ref[0][:, :1], (TG, JALL))

        def block(s, carry):
            p1, p2, e = carry
            shift = lax.rem(LCHUNK - s * 16, LCHUNK)
            fs = pltpu.roll(f_ref[0], shift, 1)
            hs = pltpu.roll(h_ref[0], shift, 1)
            for u in range(16):
                if u % 8 == 0:
                    big = jnp.abs(p1) > 2.0**24
                    p1 = jnp.where(big, p1 * 2.0**-48, p1)
                    p2 = jnp.where(big, p2 * 2.0**-48, p2)
                    e = jnp.where(big, e + 48.0, e)
                    scale = jnp.exp2(jnp.maximum(e, -200.0))
                degree = (lc * LCHUNK + s * 16 + u).astype(F32)
                step = (fs[:, u : u + 1] * x) * p1 - hs[:, u : u + 1] * p2
                new = jnp.where(orders == degree, p0_ref[0], step)
                p1, p2 = new, p1
                value = new * scale
                for b in range(JALL // 128):
                    rows_s[b, pl.ds(pl.multiple_of((s * 16 + u) * TG, TG), TG), :] = value[
                        :, b * 128 : b * 128 + 128
                    ]
            return p1, p2, e

        p1, p2, e = lax.fori_loop(0, LCHUNK // 16, block, (p1_s[...], p2_s[...], e_s[...]))
        p1_s[...] = p1
        p2_s[...] = p2
        e_s[...] = e
        for t in range(TG):
            for b in range(JALL // 128):
                o_ref[t, :, b * 128 : b * 128 + 128] = rows_s[
                    b, pl.ds(t, LCHUNK, stride=TG), :
                ].astype(BF16)


def legendre_tables(lat):
    order = (lat + LAT * jnp.arange(GROUPS * TG, dtype=jnp.int32)).astype(F32)[:, None]
    degrees = jnp.arange(LPAD, dtype=F32)[None, :]

    def factor_at(degree):
        inside = degree > order
        top = jnp.where(inside, 4.0 * degree * degree - 1.0, 1.0)
        low = jnp.where(inside, degree * degree - order * order, 1.0)
        return jnp.sqrt(top / low), inside

    factor, inside = factor_at(degrees)
    earlier, earlier_inside = factor_at(degrees - 1.0)
    forward = jnp.where(inside, factor, 0.0).reshape(GROUPS, TG, LPAD)
    back = jnp.where(earlier_inside, factor / earlier, 0.0).reshape(GROUPS, TG, LPAD)
    start_log = 0.5 * (
        lax.lgamma(order + 1.5) - lax.lgamma(jnp.float32(1.5)) - lax.lgamma(order + 1.0)
    ) - 0.5 * math.log(4.0 * math.pi)
    place = jnp.arange(JALL, dtype=jnp.int32)
    cycle = place // JPAD * JLOC + jnp.minimum(place % JPAD, JLOC - 1)
    theta = (cycle.astype(F32) + 0.5) * (math.pi / (JLOC * LAT))
    start = (start_log + order * jnp.log(jnp.sin(theta))[None, :]) * (1.0 / math.log(2.0))
    exponent = jnp.floor(start)
    real = (place % JPAD < JLOC)[None, :]
    mantissa = jnp.where(real, jnp.exp2(start - exponent), 0.0)
    orders = jnp.broadcast_to(order, (GROUPS * TG, 128)).reshape(GROUPS, TG, 128)
    return pl.pallas_call(
        legendre_kernel,
        grid=(GROUPS, LPAD // LCHUNK),
        out_shape=jax.ShapeDtypeStruct((GROUPS * TG, LPAD, JALL), BF16),
        in_specs=[
            pl.BlockSpec((1, TG, 128), lambda g, lc: (g, 0, 0)),
            pl.BlockSpec((1, TG, LCHUNK), lambda g, lc: (g, 0, lc)),
            pl.BlockSpec((1, TG, LCHUNK), lambda g, lc: (g, 0, lc)),
            pl.BlockSpec((1, JALL), lambda g, lc: (0, 0)),
            pl.BlockSpec((1, TG, JALL), lambda g, lc: (g, 0, 0)),
            pl.BlockSpec((1, TG, JALL), lambda g, lc: (g, 0, 0)),
        ],
        out_specs=pl.BlockSpec((TG, LCHUNK, JALL), lambda g, lc: (g, lc, 0)),
        scratch_shapes=[pltpu.VMEM((TG, JALL), F32)] * 3 + [
            pltpu.VMEM((JALL // 128, LCHUNK * TG, 128), F32)
        ],
        compiler_params=params(32),
        cost_estimate=cost(2.5e10, 4e7),
        name="legendre_tables",
    )(
        orders,
        forward,
        back,
        jnp.cos(theta)[None, :],
        mantissa.reshape(GROUPS, TG, JALL),
        exponent.reshape(GROUPS, TG, JALL),
    )


def spectral_body(p_ref, z_ref, w_ref, sign, o_ref, s_ref, u_ref):
    z = z_ref[:, 0].reshape(JALL, 128).astype(F32)
    lane = lax.broadcasted_iota(jnp.int32, z.shape, 1) % TG
    for t in range(TG):
        part = jnp.dot(
            p_ref[t], jnp.where(lane == t, z, 0.0).astype(BF16), preferred_element_type=F32
        )
        s_ref[...] = part if t == 0 else s_ref[...] + part
    found = s_ref[...].T.reshape(CH, 2, TG, LPAD)
    real, imag = found[:, 0], found[:, 1]
    cross = w_ref[1] * sign
    kept = jnp.stack([w_ref[0] * real - cross * imag, w_ref[0] * imag + cross * real], axis=1)
    kept = kept.reshape(128, LPAD)
    row = lax.broadcasted_iota(jnp.int32, kept.shape, 0) % TG
    for t in range(TG):
        part = jnp.dot(
            jnp.where(row == t, kept, 0.0).astype(BF16), p_ref[t], preferred_element_type=F32
        )
        u_ref[...] = part if t == 0 else u_ref[...] + part
    o_ref[:, 0] = u_ref[...].T.astype(BF16).reshape(LAT, JPAD, 128)
    return real, imag


def forward_kernel(p_ref, z_ref, w_ref, o_ref, a_ref, s_ref, u_ref):
    real, imag = spectral_body(p_ref, z_ref, w_ref, 1.0, o_ref, s_ref, u_ref)
    a_ref[0, 0] = real
    a_ref[0, 1] = imag


def backward_kernel(p_ref, z_ref, w_ref, a_ref, o_ref, g_ref, s_ref, u_ref):
    real, imag = spectral_body(p_ref, z_ref, w_ref, -1.0, o_ref, s_ref, u_ref)
    first, second = a_ref[0, 0], a_ref[0, 1]

    @pl.when(pl.program_id(0) == 0)
    def _():
        g_ref[...] = jnp.zeros_like(g_ref)

    g_ref[0] += first * real + second * imag
    g_ref[1] += first * imag - second * real


def spectral_stage(kernel, tables, spectra, weights, extra_in, extra_out):
    wave_spec = pl.BlockSpec((LAT, 1, JPAD, 128), lambda g: (0, g, 0, 0))
    return pl.pallas_call(
        kernel,
        grid=(GROUPS,),
        out_shape=(jax.ShapeDtypeStruct((LAT, GROUPS, JPAD, 128), BF16), extra_out[0]),
        in_specs=[
            pl.BlockSpec((TG, LPAD, JALL), lambda g: (g, 0, 0)),
            wave_spec,
            pl.BlockSpec((2, CH, TG, LPAD), lambda g: (0, 0, 0, 0)),
        ]
        + [spec for _, spec in extra_in],
        out_specs=(wave_spec, extra_out[1]),
        scratch_shapes=[pltpu.VMEM((LPAD, 128), F32), pltpu.VMEM((128, JALL), F32)],
        compiler_params=params(48),
        cost_estimate=cost(1.2e10, 4.2e7),
        name="spectral_stage",
    )(tables, spectra, weights, *[value for value, _ in extra_in])


def fourier_table():
    kappa = jnp.arange(KDIM, dtype=jnp.int32)
    block = kappa // 128 * 8 + kappa % 8
    local = block % NT * 16 + kappa // 8 % 16
    point = (block // NT * NLOC + local)[:, None]
    real = (local < NLOC)[:, None]
    mu = jnp.arange(MUDIM, dtype=jnp.int32)
    lat = mu // 128 * 2 + mu // 64 % 2
    wave = (lat + LAT * (mu // 16 % 4 * TG + mu % TG))[None, :]
    quarter = (mu // 8 % 2 * (POINTS // 4))[None, :]
    phase = (wave * point + quarter) % POINTS
    values = jnp.cos(phase.astype(F32) * (2.0 * math.pi / POINTS))
    return jnp.where(real, values, 0.0).astype(BF16), wave


def swap(values, axis):
    return lax.all_to_all(values, axis, 0, 0, tiled=True)


def per_device(field, cotangent, spectral_filter):
    lat = lax.axis_index("lat")
    spacing = 2.0 * math.pi / POINTS
    table, wave = fourier_table()
    doubling = jnp.where(wave == 0, 1.0, 2.0).astype(F32)
    plain = jnp.ones((1, MUDIM), F32)
    theta = ((lat * JLOC + jnp.arange(JPAD)).astype(F32) + 0.5) * (math.pi / (JLOC * LAT))
    quadrature = jnp.broadcast_to(
        (spacing * math.pi / (JLOC * LAT) * jnp.sin(theta))[:, None], (JPAD, 128)
    )
    ones = jnp.ones((JPAD, 128), F32)
    tables = legendre_tables(lat)
    weights = jnp.pad(
        jnp.transpose(spectral_filter.astype(F32), (0, 2, 1)), ((0, 0), (0, 0), (0, LPAD - DEG))
    )
    weights = jnp.broadcast_to(weights[:, :, None, :], (2, CH, TG, LPAD))

    field_shares = swap(to_shares(field), "lon")
    cot_shares = swap(to_shares(cotangent), "lon")
    field_waves = swap(to_waves(field_shares, table, quadrature, plain), "lat")
    cot_waves = swap(to_waves(cot_shares, table, ones, doubling), "lat")

    analysis_spec = pl.BlockSpec((1, 2, CH, TG, LPAD), lambda g: (g, 0, 0, 0, 0))
    out_waves, analysis = spectral_stage(
        forward_kernel,
        tables,
        field_waves,
        weights,
        [],
        (jax.ShapeDtypeStruct((GROUPS, 2, CH, TG, LPAD), F32), analysis_spec),
    )
    grad_waves, terms = spectral_stage(
        backward_kernel,
        tables,
        cot_waves,
        weights,
        [(analysis, analysis_spec)],
        (
            jax.ShapeDtypeStruct((2, CH, TG, LPAD), F32),
            pl.BlockSpec((2, CH, TG, LPAD), lambda g: (0, 0, 0, 0)),
        ),
    )
    output = from_shares(
        swap(from_waves(swap(out_waves, "lat"), table, ones, doubling), "lon")
    )
    grad_field = from_shares(
        swap(from_waves(swap(grad_waves, "lat"), table, quadrature, plain), "lon")
    )
    summed = jnp.sum(terms, axis=2)
    for bit in range(4):
        pairs = [(i, i ^ (1 << bit)) for i in range(LAT)]
        summed = summed + lax.ppermute(summed, "lat", pairs)
    grad_filter = jnp.transpose(summed[:, :, :DEG], (0, 2, 1))
    return (output, grad_field, grad_filter)


def solution(mesh):
    in_specs = (P("lon", "lat", None), P("lon", "lat", None), P(None, None, "lon"))
    out_specs = (P("lon", "lat", None), P("lon", "lat", None), P(None, None, "lon"))
    return jax.shard_map(
        per_device, mesh=mesh, in_specs=in_specs, out_specs=out_specs, check_vma=False
    )
```

time: 781 us -> 394 us (0.50)
  waiting for transfers between devices: 357 us -> 64.9 us
  Pallas kernels: 0 us -> 201 us
  local copies, waits for them, and re-layouts: 114 us -> 14.3 us
  blocking collectives: 75.4 us -> 0 us
  other arithmetic: 75 us -> 27.5 us
  starting transfers between devices: 116 us -> 82 us
  matrix products: 20.6 us -> 0 us
  between operations: 18.1 us -> 0.93 us
    psum x1 -> x0, waiting for transfers between devices: 284 us -> none  [per_device(): summed = lax.psum(gradient_term, ('lat', 'lon'))]
    pallas_call x0 -> x11, Pallas kernels: none -> 201 us  [the longest x2 59.2 us: spectral_stage(): pl.pallas_call(kernel, grid=(GROUPS,), out_shape=(jax.ShapeDtypeStruct((L...]
    all_gather x1 -> x0, blocking collectives: 75.4 us -> none  [per_device(): lax.all_gather(spectral_filter, 'lon', axis=2, tiled=True)]
    all_to_all x12 -> x8, starting transfers between devices: 116 us -> 67.2 us  [swap(): return lax.all_to_all(values, axis, 0, 0, tiled=True)]
    all_to_all x12 -> x8, waiting for transfers between devices: 72.6 us -> 38.4 us  [swap(): return lax.all_to_all(values, axis, 0, 0, tiled=True)]
    reshape x13 -> x0, local copies, waits for them, and re-layouts: 30 us -> none  [the longest x4 10.1 us: cycle_blocks(): return spectra.reshape(1, 1, 2, lat_count, lon_count, share_width)]
    another operation x18 -> x0, local copies, waits for them, and re-layouts: 28.7 us -> none  [the longest x17 21.3 us: legendre_pair(): log_scale = jnp.stack(log_parts, axis=1).reshape(degree_count, lat_count)]
    all_to_all x16 -> x0, local copies, waits for them, and re-layouts: 27.3 us -> none  [the longest x6 13.8 us: to_columns(): lax.all_to_all(grid_values.reshape(lon_local, lat_local * channels), 'lon...]
  transfers between devices with their start and end apart: 13 -> 12, of which waited for: 7 -> 6; matrix products, arithmetic and copies ran while one was open for 22% -> 7% of each run, Pallas kernels for 0% -> 49%
where the time goes in v1:
time: 394 us; the launch traced here: 390 us
  Pallas kernels  201 us (51%)
  starting transfers between devices  82 us (21%)
  waiting for transfers between devices  64.9 us (16%)
  other arithmetic  27.5 us (7%)
  local copies, waits for them, and re-layouts  14.3 us (4%)
    all_to_all x8, starting transfers between devices, swap(): return lax.all_to_all(values, axis, 0, 0, tiled=True)  67.2 us
    pallas_call x2, Pallas kernels, spectral_stage(): pl.pallas_call(kernel, grid=(GROUPS,), out_shape=(jax.ShapeDtypeStruct((L...  59.2 us
    pallas_call x1, Pallas kernels, legendre_tables(): pl.pallas_call(legendre_kernel, grid=(GROUPS, LPAD // LCHUNK), out_shape=...  55.6 us
    all_to_all x8, waiting for transfers between devices, swap(): return lax.all_to_all(values, axis, 0, 0, tiled=True)  38.4 us
    pallas_call x2, Pallas kernels, from_waves(): pl.pallas_call(inverse_kernel, out_shape=jax.ShapeDtypeStruct((LON * NT,...  33.4 us
    pallas_call x2, Pallas kernels, to_waves(): pl.pallas_call(fourier_kernel, out_shape=jax.ShapeDtypeStruct((LAT, GROUP...  33.1 us
    ppermute x4, waiting for transfers between devices, per_device(): summed = summed + lax.ppermute(summed, 'lat', pairs)  26.4 us
    convert_element_type x1, other arithmetic, fourier_table(): return (jnp.where(real, values, 0.0).astype(BF16), wave)  26.2 us
  transfers between devices with their start and end apart: 12, of which 6 were waited for; matrix products, arithmetic and copies ran while one was open for 7% of the time, Pallas kernels for 49%

profile of v1, /device:TPU:1, one launch (start us, length us, event | category | flops | bytes accessed | tf_op | source)
XLA Modules:
  0.0 390.4 jit_solution(11331220577925594516)
XLA Ops:
  0.6 1.3 pad.14.x_ref
  2.0 4.1 %to_shares.2 = bf16[32,3,48,128]{3,2,1,0:T(8,128)(2,1)} custom-call(bf16[48,48,256]{2,1,0:T(8,128)(2,1)S(1)} %pad.14.x_ref), custom_call_target="tpu_custom_call" | custom-call | flops 10000000 | bytes 2400000 | tf_op jit(solution)/shard_map/to_shares/pallas_call | solution.py:68
  6.1 16.6 %all-to-all-start = ((bf16[32,3,48,128]{3,2,1,0:T(8,128)(2,1)}), bf16[32,3,48,128]{3,2,1,0:T(8,128)(2,1)}, u32[]{:S(2)}, u32[]{:S(2)}) async-start(bf16[32,3,48,128]{3,2,1,0:T(8,128)(2,1)} %to_shares.2), calls=%async_computation | async-start | bytes 2359296 | tf_op jit(solution)/shard_map/all_to_all | solution.py:392
  22.7 1.3 pad.17.x_ref
  24.0 4.1 %to_shares.3 = bf16[32,3,48,128]{3,2,1,0:T(8,128)(2,1)} custom-call(bf16[48,48,256]{2,1,0:T(8,128)(2,1)S(1)} %pad.17.x_ref), custom_call_target="tpu_custom_call" | custom-call | flops 10000000 | bytes 2400000 | tf_op jit(solution)/shard_map/to_shares/pallas_call | solution.py:68
  28.1 25.1 %all-to-all-done = bf16[32,3,48,128]{3,2,1,0:T(8,128)(2,1)} async-done(((bf16[32,3,48,128]{3,2,1,0:T(8,128)(2,1)}), bf16[32,3,48,128]{3,2,1,0:T(8,128)(2,1)}, u32[]{:S(2)}, u32[]{:S(2)}) %all-to-all-start) | async-done | bytes 1179680 | tf_op jit(solution)/shard_map/all_to_all | solution.py:392
  53.2 8.4 %all-to-all-start.4 = ((bf16[32,3,48,128]{3,2,1,0:T(8,128)(2,1)}), bf16[32,3,48,128]{3,2,1,0:T(8,128)(2,1)}, u32[]{:S(2)}, u32[]{:S(2)}) async-start(bf16[32,3,48,128]{3,2,1,0:T(8,128)(2,1)} %to_shares.3), calls=%async_computation.4 | async-start | bytes 2359296 | tf_op jit(solution)/shard_map/all_to_all | solution.py:392
  61.7 26.2 %fusion.4.f_ref = bf16[1536,1024]{1,0:T(8,128)(2,1)S(1)} fusion(s32[1024]{0:T(1024)S(1)} %get-tuple-element.26, s32[1536]{0:T(1024)S(1)} %fusion.30, s32[1024]{0:T(1024)S(1)} %get-tuple-element.25, pred[1536]{0:T(1024)(128)(4,1)S(1)} %broadcast_compare_fusion), kind=kLoop, calls=%fused_computation.5 | loop fusion | flops 18874368 | bytes 3161600 | tf_op jit(solution)/shard_map/convert_element_type | solution.py:388
  88.0 16.6 %to_waves.2 = bf16[16,4,48,128]{3,2,1,0:T(8,128)(2,1)S(1)} custom-call(bf16[96,48,128]{2,1,0:T(8,128)(2,1)} %bitcast.x_ref, bf16[1536,1024]{1,0:T(8,128)(2,1)S(1)} %fusion.4.f_ref, f32[48,128]{1,0:T(8,128)S(1)} %broadcast_in_dim.99.row_ref, f32[1,1024]{1,0:T(1,128)S(1)} %broadcast_in_dim.100.lane_ref), custom_call_target="tpu_custom_call" | custom-call | flops 1207959552 | bytes 5000000 | tf_op jit(solution)/shard_map/to_waves/pallas_call | solution.py:138
  106.0 6.6 %all-to-all-start.1 = ((bf16[16,4,48,128]{3,2,1,0:T(8,128)(2,1)}), bf16[16,4,48,128]{3,2,1,0:T(8,128)(2,1)}, u32[]{:S(2)}, u32[]{:S(2)}) async-start(bf16[16,4,48,128]{3,2,1,0:T(8,128)(2,1)} %copy-done.2), calls=%async_computation.1 | async-start | bytes 1572864 | tf_op jit(solution)/shard_map/all_to_all | solution.py:392
  113.2 16.6 %to_waves.3 = bf16[16,4,48,128]{3,2,1,0:T(8,128)(2,1)S(1)} custom-call(bf16[96,48,128]{2,1,0:T(8,128)(2,1)} %bitcast.3.x_ref, bf16[1536,1024]{1,0:T(8,128)(2,1)S(1)} %fusion.4.f_ref, f32[48,128]{1,0:T(8,128)S(1)} %broadcast_in_dim.102.row_ref, f32[1,1024]{1,0:T(1,128)S(1)} %compare_select_fusion.7.lane_ref), custom_call_target="tpu_custom_call" | custom-call | flops 1207959552 | bytes 5000000 | tf_op jit(solution)/shard_map/to_waves/pallas_call | solution.py:138
  131.2 5.7 %all-to-all-start.5 = ((bf16[16,4,48,128]{3,2,1,0:T(8,128)(2,1)}), bf16[16,4,48,128]{3,2,1,0:T(8,128)(2,1)}, u32[]{:S(2)}, u32[]{:S(2)}) async-start(bf16[16,4,48,128]{3,2,1,0:T(8,128)(2,1)} %copy-done.3), calls=%async_computation.5 | async-start | bytes 1572864 | tf_op jit(solution)/shard_map/all_to_all | solution.py:392
  137.0 55.6 %legendre_tables.1.p_ref = bf16[32,768,768]{2,1,0:T(8,128)(2,1)} custom-call(f32[4,8,128]{2,1,0:T(8,128)S(1)} %broadcast_in_dim.91.m_ref, f32[4,8,768]{2,1,0:T(8,128)S(1)} %get-tuple-element.15.f_ref, f32[4,8,768]{2,1,0:T(8,128)S(1)} %get-tuple-element.16.h_ref, f32[1,768]{1,0:T(1,128)S(1)} %fusion.84.x_ref, f32[4,8,768]{2,1,0:T(8,128)S(1)} %get-tuple-element.14.p0_ref, ...), custom_call_target="tpu_custom_call" | custom-call | flops 24999999488 | bytes 40000000 | tf_op jit(solution)/shard_map/legendre_tables/pallas_call | solution.py:286
  192.7 29.4 %spectral_stage.2 = (bf16[16,4,48,128]{3,2,1,0:T(8,128)(2,1)S(1)}, f32[4,2,8,8,768]{4,3,2,1,0:T(8,128)S(1)}) custom-call(bf16[32,768,768]{2,1,0:T(8,128)(2,1)} %legendre_tables.1.p_ref, bf16[16,4,48,128]{3,2,1,0:T(8,128)(2,1)} %all-to-all-done.1.z_ref, f32[2,8,8,768]{3,2,1,0:T(8,128)S(1)} %broadcast_in_dim.101.w_ref), custom_call_target="tpu_custom_call" | custom-call | flops 12000000000 | bytes 42000000 | tf_op jit(solution)/shard_map/spectral_stage/pallas_call | solution.py:358
  224.1 5.7 %all-to-all-start.2 = ((bf16[16,4,48,128]{3,2,1,0:T(8,128)(2,1)}), bf16[16,4,48,128]{3,2,1,0:T(8,128)(2,1)}, u32[]{:S(2)}, u32[]{:S(2)}) async-start(bf16[16,4,48,128]{3,2,1,0:T(8,128)(2,1)} %copy-done.5), calls=%async_computation.2 | async-start | bytes 1572864 | tf_op jit(solution)/shard_map/all_to_all | solution.py:392
  229.8 1.4 copy-done.13
  231.2 29.8 %spectral_stage.3 = (bf16[16,4,48,128]{3,2,1,0:T(8,128)(2,1)S(1)}, f32[2,8,8,768]{3,2,1,0:T(8,128)S(1)}) custom-call(bf16[32,768,768]{2,1,0:T(8,128)(2,1)} %legendre_tables.1.p_ref, bf16[16,4,48,128]{3,2,1,0:T(8,128)(2,1)} %all-to-all-done.5.z_ref, f32[2,8,8,768]{3,2,1,0:T(8,128)S(1)} %broadcast_in_dim.101.w_ref, f32[4,2,8,8,768]{4,3,2,1,0:T(8,128)S(1)} %copy-done.13), custom_call_target="tpu_custom_call" | custom-call | flops 12000000000 | bytes 42000000 | tf_op jit(solution)/shard_map/spectral_stage/pallas_call | solution.py:358
  262.6 5.7 %all-to-all-start.6 = ((bf16[16,4,48,128]{3,2,1,0:T(8,128)(2,1)}), bf16[16,4,48,128]{3,2,1,0:T(8,128)(2,1)}, u32[]{:S(2)}, u32[]{:S(2)}) async-start(bf16[16,4,48,128]{3,2,1,0:T(8,128)(2,1)} %copy-done.4), calls=%async_computation.6 | async-start | bytes 1572864 | tf_op jit(solution)/shard_map/all_to_all | solution.py:392
  269.1 16.7 %from_waves.2 = bf16[96,48,128]{2,1,0:T(8,128)(2,1)S(1)} custom-call(bf16[16,4,48,128]{3,2,1,0:T(8,128)(2,1)} %all-to-all-done.2.v_ref, bf16[1536,1024]{1,0:T(8,128)(2,1)S(1)} %fusion.4.f_ref, f32[48,128]{1,0:T(8,128)S(1)} %copy-done.11, f32[1,1024]{1,0:T(1,128)S(1)} %compare_select_fusion.7.lane_ref), custom_call_target="tpu_custom_call" | custom-call | flops 1207959552 | bytes 5000000 | tf_op jit(solution)/shard_map/from_waves/pallas_call | solution.py:191
  286.8 11.9 %all-to-all-start.3 = ((bf16[32,3,48,128]{3,2,1,0:T(8,128)(2,1)}), bf16[32,3,48,128]{3,2,1,0:T(8,128)(2,1)}, u32[]{:S(2)}, u32[]{:S(2)}) async-start(bf16[32,3,48,128]{3,2,1,0:T(8,128)(2,1)} %bitcast.8), calls=%async_computation.3 | async-start | bytes 2359296 | tf_op jit(solution)/shard_map/all_to_all | solution.py:392
  299.5 16.7 %from_waves.3 = bf16[96,48,128]{2,1,0:T(8,128)(2,1)S(1)} custom-call(bf16[16,4,48,128]{3,2,1,0:T(8,128)(2,1)} %all-to-all-done.6.v_ref, bf16[1536,1024]{1,0:T(8,128)(2,1)S(1)} %fusion.4.f_ref, f32[48,128]{1,0:T(8,128)S(1)} %copy-done.9, f32[1,1024]{1,0:T(1,128)S(1)} %broadcast_in_dim.100.lane_ref), custom_call_target="tpu_custom_call" | custom-call | flops 1207959552 | bytes 5000000 | tf_op jit(solution)/shard_map/from_waves/pallas_call | solution.py:191
  317.2 13.4 %all-to-all-done.3.x_ref = bf16[32,3,48,128]{3,2,1,0:T(8,128)(2,1)} async-done(((bf16[32,3,48,128]{3,2,1,0:T(8,128)(2,1)}), bf16[32,3,48,128]{3,2,1,0:T(8,128)(2,1)}, u32[]{:S(2)}, u32[]{:S(2)}) %all-to-all-start.3) | async-done | bytes 1179680 | tf_op jit(solution)/shard_map/all_to_all | solution.py:392
  330.6 6.4 %all-to-all-start.7 = ((bf16[32,3,48,128]{3,2,1,0:T(8,128)(2,1)}), bf16[32,3,48,128]{3,2,1,0:T(8,128)(2,1)S(1)}, u32[]{:S(2)}, u32[]{:S(2)}) async-start(bf16[32,3,48,128]{3,2,1,0:T(8,128)(2,1)} %bitcast.7), calls=%async_computation.7 | async-start | bytes 2359296 | tf_op jit(solution)/shard_map/all_to_all | solution.py:392
  337.2 4.6 %collective-permute-start = (f32[2,8,768]{2,1,0:T(8,128)S(1)}, f32[2,8,768]{2,1,0:T(8,128)S(1)}, u32[]{:S(2)}, u32[]{:S(2)}) collective-permute-start(f32[2,8,768]{2,1,0:T(8,128)S(1)} %reduce_sum.9), channel_id=1, source_target_pairs={{0,32},{32,0},{64,96},{96,64},{128,160},{160,128},{192,224},{224,1... | collective-permute-start | bytes 147464 | tf_op jit(solution)/shard_map/ppermute | solution.py:446
  342.6 2.6 collective-permute-start.1
  345.2 22.1 %collective-permute-done.1 = f32[2,8,768]{2,1,0:T(8,128)S(1)} collective-permute-done((f32[2,8,768]{2,1,0:T(8,128)S(1)}, f32[2,8,768]{2,1,0:T(8,128)S(1)}, u32[]{:S(2)}, u32[]{:S(2)}) %collective-permute-start.1) | collective-permute-done | bytes 49184 | tf_op jit(solution)/shard_map/ppermute | solution.py:446
  367.3 3.0 collective-permute-start.2
  370.3 1.8 collective-permute-done.2
  372.1 4.6 %collective-permute-start.3 = (f32[2,8,768]{2,1,0:T(8,128)S(1)}, f32[2,8,768]{2,1,0:T(8,128)S(1)}, u32[]{:S(2)}, u32[]{:S(2)}) collective-permute-start(f32[2,8,768]{2,1,0:T(8,128)S(1)} %add.598), channel_id=1, source_target_pairs={{0,256},{32,288},{64,320},{96,352},{128,384},{160,416},{192,448},{... | collective-permute-start | bytes 147464 | tf_op jit(solution)/shard_map/ppermute | solution.py:446
  376.8 1.7 collective-permute-done.3
  379.1 6.3 %from_shares.2 = bf16[45,45,256]{2,1,0:T(8,128)(2,1)} custom-call(bf16[32,3,48,128]{3,2,1,0:T(8,128)(2,1)} %all-to-all-done.3.x_ref), custom_call_target="tpu_custom_call" | custom-call | flops 10000000 | bytes 2400000 | tf_op jit(solution)/shard_map/from_shares/pallas_call | solution.py:95
  385.4 5.0 %from_shares.3 = bf16[45,45,256]{2,1,0:T(8,128)(2,1)} custom-call(bf16[32,3,48,128]{3,2,1,0:T(8,128)(2,1)S(1)} %all-to-all-done.7.x_ref), custom_call_target="tpu_custom_call" | custom-call | flops 10000000 | bytes 2400000 | tf_op jit(solution)/shard_map/from_shares/pallas_call | solution.py:95
  (60 shorter events, 12.5 us)
Async XLA Ops:
  6.1 47.1 %all-to-all-start = ((bf16[32,3,48,128]{3,2,1,0:T(8,128)(2,1)}), bf16[32,3,48,128]{3,2,1,0:T(8,128)(2,1)}, u32[]{:S(2)}, u32[]{:S(2)}) async-start(bf16[32,3,48,128]{3,2,1,0:T(8,128)(2,1)} %to_shares.2), calls=%async_computation | async-start | bytes 2359296 | tf_op jit(solution)/shard_map/all_to_all | solution.py:392
  53.2 52.8 %all-to-all-start.4 = ((bf16[32,3,48,128]{3,2,1,0:T(8,128)(2,1)}), bf16[32,3,48,128]{3,2,1,0:T(8,128)(2,1)}, u32[]{:S(2)}, u32[]{:S(2)}) async-start(bf16[32,3,48,128]{3,2,1,0:T(8,128)(2,1)} %to_shares.3), calls=%async_computation.4 | async-start | bytes 2359296 | tf_op jit(solution)/shard_map/all_to_all | solution.py:392
  104.5 0.9 copy-start.2
  105.4 0.6 copy-start.8
  106.0 25.2 %all-to-all-start.1 = ((bf16[16,4,48,128]{3,2,1,0:T(8,128)(2,1)}), bf16[16,4,48,128]{3,2,1,0:T(8,128)(2,1)}, u32[]{:S(2)}, u32[]{:S(2)}) async-start(bf16[16,4,48,128]{3,2,1,0:T(8,128)(2,1)} %copy-done.2), calls=%async_computation.1 | async-start | bytes 1572864 | tf_op jit(solution)/shard_map/all_to_all | solution.py:392
  129.8 0.9 copy-start.3
  130.6 0.6 copy-start.10
  131.2 92.8 %all-to-all-start.5 = ((bf16[16,4,48,128]{3,2,1,0:T(8,128)(2,1)}), bf16[16,4,48,128]{3,2,1,0:T(8,128)(2,1)}, u32[]{:S(2)}, u32[]{:S(2)}) async-start(bf16[16,4,48,128]{3,2,1,0:T(8,128)(2,1)} %copy-done.3), calls=%async_computation.5 | async-start | bytes 1572864 | tf_op jit(solution)/shard_map/all_to_all | solution.py:392
  137.0 55.6 %copy-start.14 = (bf16[2,720,8]{1,2,0:T(8,128)(2,1)S(1)}, bf16[2,720,8]{1,2,0:T(8,128)(2,1)}, u32[]{:S(2)}) copy-start(bf16[2,720,8]{1,2,0:T(8,128)(2,1)} %param.5) | copy-start | bytes 69124
  222.1 0.9 copy-start.5
  222.9 1.1 copy-start.12
  224.1 38.6 %all-to-all-start.2 = ((bf16[16,4,48,128]{3,2,1,0:T(8,128)(2,1)}), bf16[16,4,48,128]{3,2,1,0:T(8,128)(2,1)}, u32[]{:S(2)}, u32[]{:S(2)}) async-start(bf16[16,4,48,128]{3,2,1,0:T(8,128)(2,1)} %copy-done.5), calls=%async_computation.2 | async-start | bytes 1572864 | tf_op jit(solution)/shard_map/all_to_all | solution.py:392
  229.8 1.4 copy-start.13
  261.0 0.9 copy-start.4
  261.9 0.7 copy-start.6
  262.6 24.1 %all-to-all-start.6 = ((bf16[16,4,48,128]{3,2,1,0:T(8,128)(2,1)}), bf16[16,4,48,128]{3,2,1,0:T(8,128)(2,1)}, u32[]{:S(2)}, u32[]{:S(2)}) async-start(bf16[16,4,48,128]{3,2,1,0:T(8,128)(2,1)} %copy-done.4), calls=%async_computation.6 | async-start | bytes 1572864 | tf_op jit(solution)/shard_map/all_to_all | solution.py:392
  268.4 0.7 copy-start.11
  285.8 1.0 copy-start.1
  286.8 43.8 %all-to-all-start.3 = ((bf16[32,3,48,128]{3,2,1,0:T(8,128)(2,1)}), bf16[32,3,48,128]{3,2,1,0:T(8,128)(2,1)}, u32[]{:S(2)}, u32[]{:S(2)}) async-start(bf16[32,3,48,128]{3,2,1,0:T(8,128)(2,1)} %bitcast.8), calls=%async_computation.3 | async-start | bytes 2359296 | tf_op jit(solution)/shard_map/all_to_all | solution.py:392
  298.7 0.7 copy-start.9
  299.5 37.6 %copy-start.7 = (f32[2,8,8,768]{3,2,1,0:T(8,128)S(1)}, f32[2,8,8,768]{3,2,1,0:T(8,128)}, u32[]{:S(2)}) copy-start(f32[2,8,8,768]{3,2,1,0:T(8,128)} %copy-done.6) | copy-start | bytes 1179652
  316.2 1.0 copy-start
  330.6 54.8 %all-to-all-start.7 = ((bf16[32,3,48,128]{3,2,1,0:T(8,128)(2,1)}), bf16[32,3,48,128]{3,2,1,0:T(8,128)(2,1)S(1)}, u32[]{:S(2)}, u32[]{:S(2)}) async-start(bf16[32,3,48,128]{3,2,1,0:T(8,128)(2,1)} %bitcast.7), calls=%async_computation.7 | async-start | bytes 2359296 | tf_op jit(solution)/shard_map/all_to_all | solution.py:392
  337.2 5.5 %collective-permute-start = (f32[2,8,768]{2,1,0:T(8,128)S(1)}, f32[2,8,768]{2,1,0:T(8,128)S(1)}, u32[]{:S(2)}, u32[]{:S(2)}) collective-permute-start(f32[2,8,768]{2,1,0:T(8,128)S(1)} %reduce_sum.9), channel_id=1, source_target_pairs={{0,32},{32,0},{64,96},{96,64},{128,160},{160,128},{192,224},{224,1... | collective-permute-start | bytes 147464 | tf_op jit(solution)/shard_map/ppermute | solution.py:446
  342.6 24.7 %collective-permute-start.1 = (f32[2,8,768]{2,1,0:T(8,128)S(1)}, f32[2,8,768]{2,1,0:T(8,128)S(1)}, u32[]{:S(2)}, u32[]{:S(2)}) collective-permute-start(f32[2,8,768]{2,1,0:T(8,128)S(1)} %add.596), channel_id=1, source_target_pairs={{0,64},{32,96},{64,0},{96,32},{128,192},{160,224},{192,128},{224,1... | collective-permute-start | bytes 147464 | tf_op jit(solution)/shard_map/ppermute | solution.py:446
  367.3 4.8 %collective-permute-start.2 = (f32[2,8,768]{2,1,0:T(8,128)S(1)}, f32[2,8,768]{2,1,0:T(8,128)S(1)}, u32[]{:S(2)}, u32[]{:S(2)}) collective-permute-start(f32[2,8,768]{2,1,0:T(8,128)S(1)} %add.597), channel_id=1, source_target_pairs={{0,128},{32,160},{64,192},{96,224},{128,0},{160,32},{192,64},{224,... | collective-permute-start | bytes 147464 | tf_op jit(solution)/shard_map/ppermute | solution.py:446
  372.1 6.3 %collective-permute-start.3 = (f32[2,8,768]{2,1,0:T(8,128)S(1)}, f32[2,8,768]{2,1,0:T(8,128)S(1)}, u32[]{:S(2)}, u32[]{:S(2)}) collective-permute-start(f32[2,8,768]{2,1,0:T(8,128)S(1)} %add.598), channel_id=1, source_target_pairs={{0,256},{32,288},{64,320},{96,352},{128,384},{160,416},{192,448},{... | collective-permute-start | bytes 147464 | tf_op jit(solution)/shard_map/ppermute | solution.py:446
